TPU v7x, 32 devices: a whole 2x2x4 slice. The times are simulated.
32 devices in a mesh: groups: 2 (over y), dp: 8 (over z, x), cuts: 2 (over core).
Axes of the slice: x: 2, y: 2, z: 4, core: 2. Of those that a mesh axis runs over, the one named last changes fastest.
Arguments:
- activations: bfloat16 [768, 7168], P(('groups', 'dp'), 'cuts'), parts along dimension 0, may hold values from -6 to 6
- out_grads: bfloat16 [768, 4096], P(('groups', 'dp'), 'cuts'), parts along dimension 0, may hold values from -6 to 6
- counts: int32 [16, 8], P(('groups', 'dp')), parts along dimension 0, may hold values from 1 to 24, 48 in all within a row
- doc_slots: int32 [128], P('groups'), parts along dimension 0, may hold values from 0 to 63, each once
- proj_in: bfloat16 [7168, 64], P('cuts'), may hold values from -0.0625 to 0.0625
- proj_out: bfloat16 [4096, 64], P('cuts'), may hold values from -0.09375 to 0.09375
- queries: bfloat16 [512, 4096], P(None, ('dp', 'cuts')), may hold values from -0.5 to 0.5
Outputs:
- scores: float32 [512, 128], P(('dp', 'cuts'), 'groups'), parts along dimension 1
There are 2 independent parts, one for each index of `groups`. A program takes and returns all parts, laid end to end along the dimension named above; an argument that names none is the same for every part. Nothing has to cross between parts.
Inputs may be any that keep to these rules, and one draw needn't show every extreme that they name: The 8 counts of each dp index sum to 48. `doc_slots`: each document gets a different column.
All inputs are finite; a program needn't handle non-finite values.
Results may differ from a plain program's by a relative error of at most 0.0029.
Values may be sent and summed in bfloat16 or wider, within the bound.
A program may use at most 64 MiB of HBM per device.

v0:
```python
import jax
import jax.numpy as jnp
from jax import lax
from jax.sharding import PartitionSpec as P


def on_device(activations, out_grads, counts, doc_slots, proj_in, proj_out, queries):
    row_count = activations.shape[0]
    rank_size = proj_in.shape[1]
    doc_count = counts.shape[1]
    cut_count = lax.axis_size("cuts")
    data_count = lax.axis_size("dp")
    inward_part = jnp.dot(activations, proj_in, preferred_element_type=jnp.float32)
    outward_part = jnp.dot(out_grads, proj_out, preferred_element_type=jnp.float32)
    inward, outward = lax.psum((inward_part, outward_part), "cuts")
    ending = jnp.cumsum(counts[0])
    position = lax.iota(jnp.int32, row_count)
    owner_doc = jnp.sum((ending[None, :] <= position[:, None]).astype(jnp.int32), axis=1)
    member = (owner_doc[:, None] == lax.iota(jnp.int32, doc_count)[None, :]).astype(jnp.float32)
    weights = member / counts[0].astype(jnp.float32)[None, :]
    spread = (weights[:, :, None] * outward[:, None, :]).reshape(row_count, doc_count * rank_size)
    gradients = lax.dot_general(
        spread,
        inward,
        (((0,), (0,)), ((), ())),
        precision=lax.Precision.HIGHEST,
        preferred_element_type=jnp.float32,
    )
    gradients = gradients.reshape(doc_count, rank_size * rank_size).astype(jnp.bfloat16)
    slice_width = gradients.shape[1] // (cut_count * data_count)
    arranged = gradients.reshape(doc_count, data_count, cut_count, slice_width)
    picked = lax.dynamic_index_in_dim(arranged, lax.axis_index("cuts"), 2, keepdims=False).reshape(
        doc_count, data_count * slice_width
    )
    inverse = jnp.argsort(doc_slots)
    arrived = lax.all_to_all(picked, "dp", split_axis=1, concat_axis=0, tiled=True)
    ordered = jnp.take(arrived, inverse, axis=0)
    partial_value = lax.dot_general(
        queries, ordered, (((1,), (1,)), ((), ())), preferred_element_type=jnp.float32
    )
    return lax.psum_scatter(partial_value, ("dp", "cuts"), scatter_dimension=0, tiled=True)


def solution(mesh):
    placed = (
        P(("groups", "dp"), "cuts"),
        P(("groups", "dp"), "cuts"),
        P(("groups", "dp"), None),
        P("groups"),
        P("cuts", None),
        P("cuts", None),
        P(None, ("dp", "cuts")),
    )
    return jax.shard_map(
        on_device,
        mesh=mesh,
        in_specs=placed,
        out_specs=P(("dp", "cuts"), "groups"),
        check_vma=False,
    )
```

profile of v0, /device:TPU:0, one launch (start us, length us, event | category | flops | bytes accessed | tf_op | source)
XLA Modules:
  0.0 89.7 jit_solution(10809980026371094610)
XLA Ops:
  6.5 0.0 copy-start
  6.5 0.7 copy-done.4
  7.3 0.2 reduce-window.8
  7.4 0.1 convert_reduce_fusion
  7.5 0.1 convert_divide_fusion
  7.6 0.1 copy.20
  7.7 0.0 copy-done
  7.7 0.0 copy-start.3
  7.7 1.3 %fusion.5 = f32[48,64]{1,0:T(8,128)S(1)} fusion(bf16[48,3584]{1,0:T(8,128)(2,1)} %param.7, bf16[3584,64]{0,1:T(8,128)(2,1)S(1)} %copy-done), kind=kOutput, calls=%fused_computation.19 | convolution fusion | flops 22020096 | bytes 815104 | tf_op jit(solution)/shard_map/dot_general | solution.py:13
  9.0 0.0 copy-done.2
  9.0 0.2 fusion.4
  9.2 3.8 %all-reduce = (f32[48,64]{1,0:T(8,128)S(1)}, f32[48,64]{1,0:T(8,128)S(1)}) all-reduce(f32[48,64]{1,0:T(8,128)S(1)} %fusion.4, f32[48,64]{1,0:T(8,128)S(1)} %fusion.5), channel_id=1, replica_groups=mesh['groups'=2,'dp'=8,'cuts'=2] {'cuts'}, use_global_device_ids=true, to_apply=%region_3.4 | all-reduce | flops 6144 | bytes 49152 | tf_op jit(solution)/shard_map/psum | solution.py:15
  13.0 0.1 broadcast_multiply_fusion
  13.1 0.1 mul.20
  13.2 0.3 convolution_convert_fusion
  13.6 0.1 copy.21
  13.7 0.2 convert_element_type.25
  13.8 0.0 copy-start.5
  13.9 0.1 constant_dynamic-slice_fusion
  13.9 0.0 copy-start.1
  14.0 0.6 copy.28
  14.6 7.0 %all-to-all-start = ((bf16[8,8,256]{2,0,1:T(8,128)(2,1)}), bf16[8,8,256]{2,0,1:T(8,128)(2,1)S(1)}, u32[]{:S(2)}, u32[]{:S(2)}) async-start(bf16[8,8,256]{2,0,1:T(8,128)(2,1)} %bitcast.19), calls=%async_computation | async-start | bytes 65536 | tf_op jit(solution)/shard_map/all_to_all | solution.py:36
  21.6 0.0 reduce-scatter.4.cloned.1.call-start
  21.6 0.0 copy-done.5
  21.6 2.0 %sort.17 = (s32[64]{0:T(128)}, s32[64]{0:T(128)S(1)}) sort(s32[64]{0:T(128)S(1)} %copy-done.5, s32[64]{0:T(128)S(1)} %iota.15), dimensions={0}, to_apply=%region_0.0 | sort | flops 384 | bytes 1024 | tf_op jit(solution)/shard_map/jit(argsort)/sort | solution.py:35
  23.7 4.6 %all-to-all-done = bf16[8,8,256]{2,0,1:T(8,128)(2,1)S(1)} async-done(((bf16[8,8,256]{2,0,1:T(8,128)(2,1)}), bf16[8,8,256]{2,0,1:T(8,128)(2,1)S(1)}, u32[]{:S(2)}, u32[]{:S(2)}) %all-to-all-start) | async-done | bytes 32800 | tf_op jit(solution)/shard_map/all_to_all | solution.py:36
  28.3 0.7 gather_fusion
  29.0 0.0 copy-done.1
  29.0 0.2 convolution_bitcast_fusion
  29.2 0.8 copy.25
  30.0 0.0 reduce-scatter.4.cloned.1.call-update
  30.0 52.9 %reduce-scatter.4.cloned.1.call-done = f32[32,64]{1,0:T(8,128)} async-done(((f32[512,64]{1,0:T(8,128)}), f32[32,64]{1,0:T(8,128)}) %reduce-scatter.4.cloned.1.call-update) | async-done | bytes 8208 | tf_op jit(solution)/shard_map/reduce_scatter | solution.py:41
  (8 shorter events, 0.0 us)
Async XLA Ops:
  6.5 1.1 %copy-start = (bf16[3584,64]{0,1:T(8,128)(2,1)S(1)}, bf16[3584,64]{0,1:T(8,128)(2,1)}, u32[]{:S(2)}) copy-start(bf16[3584,64]{0,1:T(8,128)(2,1)} %param.11) | copy-start | bytes 1376260
  6.5 0.7 copy-start.4
  7.7 1.3 %copy-start.2 = (bf16[2048,64]{0,1:T(8,128)(2,1)S(1)}, bf16[2048,64]{0,1:T(8,128)(2,1)}, u32[]{:S(2)}) copy-start(bf16[2048,64]{0,1:T(8,128)(2,1)} %param.12) | copy-start | bytes 786436
  7.7 1.3 %copy-start.3 = (bf16[48,2048]{1,0:T(8,128)(2,1)S(1)}, bf16[48,2048]{1,0:T(8,128)(2,1)}, u32[]{:S(2)}) copy-start(bf16[48,2048]{1,0:T(8,128)(2,1)} %param.8) | copy-start | bytes 589828
  13.8 7.8 %copy-start.5 = (s32[64]{0:T(128)S(1)}, s32[64]{0:T(128)}, u32[]{:S(2)}) copy-start(s32[64]{0:T(128)} %param.10) | copy-start | bytes 772
  13.9 15.0 %copy-start.1 = (bf16[512,256]{1,0:T(8,128)(2,1)S(1)}, bf16[512,256]{1,0:T(8,128)(2,1)}, u32[]{:S(2)}) copy-start(bf16[512,256]{1,0:T(8,128)(2,1)} %param.13) | copy-start | bytes 786436
  14.6 13.7 %all-to-all-start = ((bf16[8,8,256]{2,0,1:T(8,128)(2,1)}), bf16[8,8,256]{2,0,1:T(8,128)(2,1)S(1)}, u32[]{:S(2)}, u32[]{:S(2)}) async-start(bf16[8,8,256]{2,0,1:T(8,128)(2,1)} %bitcast.19), calls=%async_computation | async-start | bytes 65536 | tf_op jit(solution)/shard_map/all_to_all | solution.py:36
  21.6 61.3 %reduce-scatter.4.cloned.1.call-start = ((), (), s32[]{:S(2)}) async-start(), calls=%async_computation.2 | async-start | bytes 278528 | tf_op jit(solution)/shard_map/reduce_scatter | solution.py:41
Sparse Core Ops, SparseCore 0:
  30.1 52.6 reduce-scatter.3
where the time goes:
time: 90 us; the launch traced here: 89.7 us
  waiting for transfers between devices  57.4 us (64%)
  between operations  13.5 us (15%)
  starting transfers between devices  7.03 us (8%)
  blocking collectives  3.8 us (4%)
  local copies, waits for them, and re-layouts  3.45 us (4%)
  other arithmetic  2.51 us (3%)
  matrix products  1.98 us (2%)
    reduce_scatter x1, waiting for transfers between devices, on_device(): lax.psum_scatter(partial_value, ('dp', 'cuts'), scatter_dimension=0, tile...  52.9 us
    all_to_all x1, starting transfers between devices, on_device(): lax.all_to_all(picked, 'dp', split_axis=1, concat_axis=0, tiled=True)  6.99 us
    all_to_all x1, waiting for transfers between devices, on_device(): lax.all_to_all(picked, 'dp', split_axis=1, concat_axis=0, tiled=True)  4.56 us
    psum x1, blocking collectives, on_device(): inward, outward = lax.psum((inward_part, outward_part), 'cuts')  3.8 us
    sort x1, other arithmetic, on_device(): inverse = jnp.argsort(doc_slots)  2.03 us
  transfers between devices with their start and end apart: 2, of which 2 were waited for; matrix products, arithmetic and copies ran while one was open for 2% of the time, Pallas kernels for 0%

commit v1 on v0

--- a/solution.py
+++ b/solution.py
@@ -1,10 +1,17 @@
+import functools
+
 import jax
 import jax.numpy as jnp
 from jax import lax
+from jax.experimental import pallas as pl
+from jax.experimental.pallas import tpu as pltpu
 from jax.sharding import PartitionSpec as P
 
-
-def on_device(activations, out_grads, counts, doc_slots, proj_in, proj_out, queries):
+LANES = 128
+MESH = pl.DeviceIdType.MESH
+
+
+def general(activations, out_grads, counts, doc_slots, proj_in, proj_out, queries):
     row_count = activations.shape[0]
     rank_size = proj_in.shape[1]
     doc_count = counts.shape[1]
@@ -13,7 +20,8 @@
     inward_part = jnp.dot(activations, proj_in, preferred_element_type=jnp.float32)
     outward_part = jnp.dot(out_grads, proj_out, preferred_element_type=jnp.float32)
     inward, outward = lax.psum((inward_part, outward_part), "cuts")
-    ending = jnp.cumsum(counts[0])
+    earlier = lax.iota(jnp.int32, doc_count)[:, None] <= lax.iota(jnp.int32, doc_count)[None, :]
+    ending = jnp.sum(jnp.where(earlier, counts[0][:, None], 0), axis=0)
     position = lax.iota(jnp.int32, row_count)
     owner_doc = jnp.sum((ending[None, :] <= position[:, None]).astype(jnp.int32), axis=1)
     member = (owner_doc[:, None] == lax.iota(jnp.int32, doc_count)[None, :]).astype(jnp.float32)
@@ -41,6 +49,231 @@
     return lax.psum_scatter(partial_value, ("dp", "cuts"), scatter_dimension=0, tiled=True)
 
 
+def split(value):
+    high = value.astype(jnp.bfloat16)
+    return high, (value - high.astype(jnp.float32)).astype(jnp.bfloat16)
+
+
+def dot(a, b):
+    return jnp.dot(a, b, preferred_element_type=jnp.float32)
+
+
+def dot_nt(a, b):
+    return lax.dot_general(a, b, (((1,), (1,)), ((), ())), preferred_element_type=jnp.float32)
+
+
+def kernel(
+    n, chunks,
+    counts_ref, slots_ref, act_hbm, grad_hbm, pin_hbm, pout_hbm, q_hbm, o_ref,
+    act, grad, pin, pout, q, mine, other, g_send, g_recv, s_send, s_recv,
+    in_sems, q_sems, pair_sems, g_send_sems, g_recv_sems, s_send_sems, s_recv_sems,
+):
+    me = lax.axis_index("dp")
+    core = lax.axis_index("cuts")
+    rows = act.shape[0]
+    rank = pin.shape[0]
+    docs = counts_ref.shape[1]
+    groups = g_recv.shape[1] // docs
+    all_docs = n * docs
+
+    loads = []
+    for a_hbm, a, p_hbm, p, count in ((act_hbm, act, pin_hbm, pin, chunks[0]), (grad_hbm, grad, pout_hbm, pout, chunks[1])):
+        size = a.shape[1] // count
+        for k in range(count):
+            at = pl.ds(k * size, size)
+            slot = len(loads)
+            pair = (
+                pltpu.make_async_copy(a_hbm.at[:, at], a.at[:, at], in_sems.at[2 * slot]),
+                pltpu.make_async_copy(p_hbm.at[:, at], p.at[:, at], in_sems.at[2 * slot + 1]),
+            )
+            for copy in pair:
+                copy.start()
+            loads.append((pair, a, p, at))
+    q_own = pltpu.make_async_copy(q_hbm.at[:, core], q.at[core], q_sems.at[0])
+    q_own.start()
+
+    barrier = pltpu.get_barrier_semaphore()
+    pl.semaphore_signal(barrier, inc=1, device_id={"cuts": 1 - core}, device_id_type=MESH)
+    for step in range(1, n):
+        pl.semaphore_signal(barrier, inc=1, device_id={"dp": lax.rem(me + step, n)}, device_id_type=MESH)
+
+    doc_of = lax.broadcasted_iota(jnp.int32, (docs, rows), 0)
+    position = lax.broadcasted_iota(jnp.int32, (docs, rows), 1)
+    first = jnp.zeros((docs, rows), jnp.int32)
+    size = jnp.ones((docs, rows), jnp.int32)
+    start = jnp.int32(0)
+    for d in range(docs):
+        here = counts_ref[0, d]
+        first = jnp.where(doc_of == d, start, first)
+        size = jnp.where(doc_of == d, here, size)
+        start = start + here
+    member = jnp.logical_and(position >= first, position < first + size)
+    weights = jnp.where(member, 1.0 / size.astype(jnp.float32), 0.0)
+    column = lax.broadcasted_iota(jnp.int32, (2 * all_docs, all_docs), 0)
+    column = jnp.where(column >= all_docs, column - all_docs, column)
+    place = jnp.where(column == slots_ref[...], 1.0, 0.0).astype(jnp.bfloat16)
+
+    inward = jnp.zeros((rows, rank), jnp.float32)
+    outward = jnp.zeros((rows, rank), jnp.float32)
+    for number, (pair, a, p, at) in enumerate(loads):
+        for copy in pair:
+            copy.wait()
+        product = dot_nt(a[:, at], p[:, at])
+        if number < chunks[0]:
+            inward = inward + product
+        else:
+            outward = outward + product
+    mine[...] = jnp.concatenate([inward, outward], axis=1)
+
+    pl.semaphore_wait(barrier, n)
+    pair_copy = pltpu.make_async_remote_copy(
+        src_ref=mine, dst_ref=other, send_sem=pair_sems.at[0], recv_sem=pair_sems.at[1],
+        device_id={"cuts": 1 - core}, device_id_type=MESH,
+    )
+    pair_copy.start()
+    q_pair = pltpu.make_async_remote_copy(
+        src_ref=q_hbm.at[:, 1 - core], dst_ref=q.at[core], send_sem=q_sems.at[1], recv_sem=q_sems.at[2],
+        device_id={"cuts": 1 - core}, device_id_type=MESH,
+    )
+    q_pair.start()
+    pair_copy.wait_recv()
+    both = mine[...] + other[...]
+
+    low = lax.broadcasted_iota(jnp.int32, (rows, 2 * rank), 1) < rank
+    turned = pltpu.roll(both, rank, 1)
+    right = (jnp.where(low, both, 0.0), jnp.where(low, 0.0, turned))
+    flipped = both.T
+    gradients = jnp.zeros((rank // 2 * docs, 2 * rank), jnp.float32)
+    for parity in range(2):
+        left = jnp.concatenate(
+            [flipped[rank + r:rank + r + 1, :] * weights for r in range(parity, rank, 2)], axis=0
+        )
+        left_high, left_low = split(left)
+        right_high, right_low = split(right[parity])
+        gradients = gradients + (dot(left_high, right_high) + (dot(left_high, right_low) + dot(left_low, right_high)))
+    g_send[...] = gradients.astype(jnp.bfloat16).reshape(g_send.shape)
+
+    g_copies = []
+    for step in range(1, n):
+        peer = lax.rem(me + step, n)
+        copy = pltpu.make_async_remote_copy(
+            src_ref=g_send.at[peer], dst_ref=g_recv.at[me],
+            send_sem=g_send_sems.at[step], recv_sem=g_recv_sems.at[step],
+            device_id={"dp": peer}, device_id_type=MESH,
+        )
+        copy.start()
+        g_copies.append(copy)
+    g_recv[me] = g_send[me]
+    q_own.wait()
+    q_pair.wait_recv()
+    for copy in g_copies:
+        copy.wait_recv()
+
+    arrived = g_recv[...].astype(jnp.float32)
+    arranged = jnp.concatenate(
+        [arrived[:, m * docs:(m + 1) * docs, :].reshape(all_docs, 2 * rank) for m in range(groups)], axis=1
+    ).astype(jnp.bfloat16)
+    ordered = dot(place, arranged).astype(jnp.bfloat16)
+    cuts, _, out_rows, width = q.shape
+    scores = jnp.zeros((n * out_rows, 2 * all_docs), jnp.float32)
+    for k in range(cuts):
+        scores = scores + dot_nt(q[k].reshape(n * out_rows, width), ordered[:, k * width:(k + 1) * width])
+    scores = scores.reshape(n, 2, out_rows // 2, 2 * all_docs)
+    first_half = lax.broadcasted_iota(jnp.int32, (n, out_rows // 2, 2 * all_docs), 2) < all_docs
+    s_send[...] = jnp.where(first_half, scores[:, 0], scores[:, 1])
+
+    s_copies = []
+    for step in range(1, n):
+        peer = lax.rem(me + step, n)
+        copy = pltpu.make_async_remote_copy(
+            src_ref=s_send.at[peer], dst_ref=s_recv.at[me],
+            send_sem=s_send_sems.at[step], recv_sem=s_recv_sems.at[step],
+            device_id={"dp": peer}, device_id_type=MESH,
+        )
+        copy.start()
+        s_copies.append(copy)
+    s_recv[me] = s_send[me]
+    for copy in s_copies:
+        copy.wait_recv()
+    total = s_recv[0]
+    for source in range(1, n):
+        total = total + s_recv[source]
+    half = out_rows // 2
+    o_ref[0:half, :] = total[:, :all_docs]
+    o_ref[half:out_rows, :] = total[:, all_docs:]
+    pair_copy.wait_send()
+    q_pair.wait_send()
+    for copy in g_copies + s_copies:
+        copy.wait_send()
+
+
+def fused(activations, out_grads, counts, doc_slots, proj_in, proj_out, queries):
+    n = lax.axis_size("dp")
+    cuts = lax.axis_size("cuts")
+    rows, rank, docs = activations.shape[0], proj_in.shape[1], counts.shape[1]
+    all_docs = n * docs
+    query_count, width = queries.shape
+    out_rows = query_count // (n * cuts)
+    block = cuts * width // LANES * docs
+    chunks = (2, 1)
+    anywhere = pl.BlockSpec(memory_space=pltpu.HBM)
+    bf16, f32 = jnp.bfloat16, jnp.float32
+    return pl.pallas_call(
+        functools.partial(kernel, n, chunks),
+        out_shape=jax.ShapeDtypeStruct((out_rows, all_docs), f32),
+        in_specs=[
+            pl.BlockSpec(memory_space=pltpu.SMEM),
+            pl.BlockSpec(memory_space=pltpu.VMEM),
+            anywhere, anywhere, anywhere, anywhere, anywhere,
+        ],
+        out_specs=pl.BlockSpec(memory_space=pltpu.VMEM),
+        scratch_shapes=[
+            pltpu.VMEM(activations.shape, bf16),
+            pltpu.VMEM(out_grads.shape, bf16),
+            pltpu.VMEM(proj_in.shape[::-1], bf16),
+            pltpu.VMEM(proj_out.shape[::-1], bf16),
+            pltpu.VMEM((cuts, n, out_rows, width), bf16),
+            pltpu.VMEM((rows, 2 * rank), f32),
+            pltpu.VMEM((rows, 2 * rank), f32),
+            pltpu.VMEM((n, block, LANES), bf16),
+            pltpu.VMEM((n, block, LANES), bf16),
+            pltpu.VMEM((n, out_rows // 2, 2 * all_docs), f32),
+            pltpu.VMEM((n, out_rows // 2, 2 * all_docs), f32),
+            pltpu.SemaphoreType.DMA((2 * sum(chunks),)),
+            pltpu.SemaphoreType.DMA((3,)),
+            pltpu.SemaphoreType.DMA((2,)),
+            pltpu.SemaphoreType.DMA((n,)),
+            pltpu.SemaphoreType.DMA((n,)),
+            pltpu.SemaphoreType.DMA((n,)),
+            pltpu.SemaphoreType.DMA((n,)),
+        ],
+        compiler_params=pltpu.CompilerParams(
+            collective_id=0, has_side_effects=True, vmem_limit_bytes=48 * 1024 * 1024
+        ),
+    )(
+        counts, doc_slots.reshape(1, all_docs), activations, out_grads, proj_in.T, proj_out.T,
+        queries.reshape(n, cuts, out_rows, width),
+    )
+
+
+def on_device(activations, out_grads, counts, doc_slots, proj_in, proj_out, queries):
+    n, cuts = lax.axis_size("dp"), lax.axis_size("cuts")
+    rank, docs = proj_in.shape[1], counts.shape[1]
+    width = queries.shape[1]
+    fits = (
+        cuts == 2
+        and 2 * rank == LANES
+        and width % LANES == 0
+        and docs % 8 == 0
+        and (cuts * width // LANES * docs) % 16 == 0
+        and 2 * n * docs == LANES
+        and queries.shape[0] % (n * cuts * 16) == 0
+        and activations.shape[0] % 16 == 0
+    )
+    body = fused if fits else general
+    return body(activations, out_grads, counts, doc_slots, proj_in, proj_out, queries)
+
+
 def solution(mesh):
     placed = (
         P(("groups", "dp"), "cuts"),

time: 90 us -> 23.6 us (0.26)
  waiting for transfers between devices: 57.4 us -> 0 us
  Pallas kernels: 0 us -> 17.2 us
  between operations: 13.5 us -> 0.02 us
  starting transfers between devices: 7.03 us -> 0 us
  blocking collectives: 3.8 us -> 0 us
  local copies, waits for them, and re-layouts: 3.45 us -> 6.1 us
  other arithmetic: 2.51 us -> 0 us
  matrix products: 1.98 us -> 0 us
    reduce_scatter x1 -> x0, waiting for transfers between devices: 52.9 us -> none  [on_device(): lax.psum_scatter(partial_value, ('dp', 'cuts'), scatter_dimension=0, tile...]
    pallas_call x0 -> x1, Pallas kernels: none -> 17.2 us  [fused(): pl.pallas_call(functools.partial(kernel, n, chunks), out_shape=jax.ShapeD...]
    all_to_all x1 -> x0, starting transfers between devices: 6.99 us -> none  [on_device(): lax.all_to_all(picked, 'dp', split_axis=1, concat_axis=0, tiled=True)]
    all_to_all x1 -> x0, waiting for transfers between devices: 4.56 us -> none  [on_device(): lax.all_to_all(picked, 'dp', split_axis=1, concat_axis=0, tiled=True)]
    unnamed x13 -> x15, local copies, waits for them, and re-layouts: 1.59 us -> 6.1 us
    psum x1 -> x0, blocking collectives: 3.8 us -> none  [on_device(): inward, outward = lax.psum((inward_part, outward_part), 'cuts')]
    sort x1 -> x0, other arithmetic: 2.03 us -> none  [on_device(): inverse = jnp.argsort(doc_slots)]
    dot_general x4 -> x0, matrix products: 1.98 us -> none  [the longest x1 1.26 us: on_device(): jnp.dot(activations, proj_in, preferred_element_type=jnp.float32)]
  transfers between devices with their start and end apart: 2 -> 0, of which waited for: 2 -> 0; matrix products, arithmetic and copies ran while one was open for 2% -> 0% of each run, Pallas kernels for 0% -> 0%
where the time goes in v1:
time: 23.6 us; the launch traced here: 23.3 us
  Pallas kernels  17.2 us (73%)
  local copies, waits for them, and re-layouts  6.1 us (26%)
    pallas_call x1, Pallas kernels, fused(): pl.pallas_call(functools.partial(kernel, n, chunks), out_shape=jax.ShapeD...  17.2 us
    unnamed x15, local copies, waits for them, and re-layouts  6.1 us

profile of v1, /device:TPU:0, one launch (start us, length us, event | category | flops | bytes accessed | tf_op | source)
XLA Modules:
  0.0 23.3 jit_solution(13528907702019507565)
XLA Ops:
  0.0 0.0 copy-start.5
  0.0 0.0 copy-start.6
  0.0 0.7 %copy-done.5 = s32[1,8]{1,0:T(1,128)S(1)} copy-done((s32[1,8]{1,0:T(1,128)S(1)}, s32[1,8]{1,0:T(1,128)}, u32[]{:S(2)}) %copy-start.5) | copy-done | bytes 56
  0.7 0.0 copy-done.6
  0.7 0.0 copy-start
  0.7 1.0 %copy-done = bf16[3584,64]{0,1:T(8,128)(2,1)S(1)} copy-done((bf16[3584,64]{0,1:T(8,128)(2,1)S(1)}, bf16[3584,64]{0,1:T(8,128)(2,1)}, u32[]{:S(2)}) %copy-start) | copy-done | bytes 458776
  1.7 0.0 copy-start.1
  1.7 1.0 %copy-done.1 = bf16[48,3584]{1,0:T(8,128)(2,1)S(1)} copy-done((bf16[48,3584]{1,0:T(8,128)(2,1)S(1)}, bf16[48,3584]{1,0:T(8,128)(2,1)}, u32[]{:S(2)}) %copy-start.1) | copy-done | bytes 344088
  2.7 0.0 copy-start.2
  2.7 0.9 %copy-done.2 = bf16[2048,64]{0,1:T(8,128)(2,1)S(1)} copy-done((bf16[2048,64]{0,1:T(8,128)(2,1)S(1)}, bf16[2048,64]{0,1:T(8,128)(2,1)}, u32[]{:S(2)}) %copy-start.2) | copy-done | bytes 262168
  3.6 0.0 copy-start.3
  3.6 0.9 %copy-done.3 = bf16[512,256]{1,0:T(8,128)(2,1)S(1)} copy-done((bf16[512,256]{1,0:T(8,128)(2,1)S(1)}, bf16[512,256]{1,0:T(8,128)(2,1)}, u32[]{:S(2)}) %copy-start.3) | copy-done | bytes 262168
  4.6 0.0 copy-start.4
  4.6 0.9 %copy-done.4 = bf16[48,2048]{1,0:T(8,128)(2,1)S(1)} copy-done((bf16[48,2048]{1,0:T(8,128)(2,1)S(1)}, bf16[48,2048]{1,0:T(8,128)(2,1)}, u32[]{:S(2)}) %copy-start.4) | copy-done | bytes 196632
  5.5 17.2 %shard_map.73 = f32[32,64]{1,0:T(8,128)S(1)} custom-call(s32[1,8]{1,0:T(1,128)S(1)} %copy-done.5, s32[1,64]{1,0:T(1,128)S(1)} %bitcast.7, bf16[48,3584]{1,0:T(8,128)(2,1)S(1)} %copy-done.1, bf16[48,2048]{1,0:T(8,128)(2,1)S(1)} %copy-done.4, bf16[64,3584]{1,0:T(8,128)(2,1)S(1)} %bitcast.4, bf16[64,2048]{1,0:T(8,128)(2,1)S(1)} %bitcast.5, ...), custom_call_target="tpu_custom_call" | custom-call | tf_op jit(solution)/shard_map/pallas_call | solution.py:221
  22.7 0.6 %copy.9 = f32[32,64]{1,0:T(8,128)} copy(f32[32,64]{1,0:T(8,128)S(1)} %shard_map.73) | data formatting | bytes 16384
Async XLA Ops:
  0.0 0.7 %copy-start.5 = (s32[1,8]{1,0:T(1,128)S(1)}, s32[1,8]{1,0:T(1,128)}, u32[]{:S(2)}) copy-start(s32[1,8]{1,0:T(1,128)} %counts_ref.1) | copy-start | bytes 100
  0.0 0.7 %copy-start.6 = (s32[64]{0:T(128)S(1)}, s32[64]{0:T(128)}, u32[]{:S(2)}) copy-start(s32[64]{0:T(128)} %param.10) | copy-start | bytes 772
  0.7 1.0 %copy-start = (bf16[3584,64]{0,1:T(8,128)(2,1)S(1)}, bf16[3584,64]{0,1:T(8,128)(2,1)}, u32[]{:S(2)}) copy-start(bf16[3584,64]{0,1:T(8,128)(2,1)} %param.11) | copy-start | bytes 1376260
  1.7 1.0 %copy-start.1 = (bf16[48,3584]{1,0:T(8,128)(2,1)S(1)}, bf16[48,3584]{1,0:T(8,128)(2,1)}, u32[]{:S(2)}) copy-start(bf16[48,3584]{1,0:T(8,128)(2,1)} %act_hbm.1) | copy-start | bytes 1032196
  2.7 0.9 %copy-start.2 = (bf16[2048,64]{0,1:T(8,128)(2,1)S(1)}, bf16[2048,64]{0,1:T(8,128)(2,1)}, u32[]{:S(2)}) copy-start(bf16[2048,64]{0,1:T(8,128)(2,1)} %param.12) | copy-start | bytes 786436
  3.6 0.9 %copy-start.3 = (bf16[512,256]{1,0:T(8,128)(2,1)S(1)}, bf16[512,256]{1,0:T(8,128)(2,1)}, u32[]{:S(2)}) copy-start(bf16[512,256]{1,0:T(8,128)(2,1)} %param.13) | copy-start | bytes 786436
  4.6 0.9 %copy-start.4 = (bf16[48,2048]{1,0:T(8,128)(2,1)S(1)}, bf16[48,2048]{1,0:T(8,128)(2,1)}, u32[]{:S(2)}) copy-start(bf16[48,2048]{1,0:T(8,128)(2,1)} %grad_hbm.1) | copy-start | bytes 589828

commit v2 on v1

--- a/solution.py
+++ b/solution.py
@@ -248,7 +248,7 @@
             pltpu.SemaphoreType.DMA((n,)),
         ],
         compiler_params=pltpu.CompilerParams(
-            collective_id=0, has_side_effects=True, vmem_limit_bytes=48 * 1024 * 1024
+            collective_id=0, has_side_effects=True, vmem_limit_bytes=60 * 1024 * 1024
         ),
     )(
         counts, doc_slots.reshape(1, all_docs), activations, out_grads, proj_in.T, proj_out.T,

time: 23.6 us -> 19.1 us (0.81)
  local copies, waits for them, and re-layouts: 6.1 us -> 1.32 us
  Pallas kernels: 17.2 us -> 17.5 us
    unnamed x15 -> x1, local copies, waits for them, and re-layouts: 6.1 us -> 1.32 us
    pallas_call x1, Pallas kernels: 17.2 us -> 17.5 us  [fused(): pl.pallas_call(functools.partial(kernel, n, chunks), out_shape=jax.ShapeD...]
where the time goes in v2:
time: 19.1 us; the launch traced here: 18.8 us
  Pallas kernels  17.5 us (92%)
  local copies, waits for them, and re-layouts  1.32 us (7%)
    pallas_call x1, Pallas kernels, fused(): pl.pallas_call(functools.partial(kernel, n, chunks), out_shape=jax.ShapeD...  17.5 us
    unnamed x1, local copies, waits for them, and re-layouts  1.32 us

profile of v2, /device:TPU:0, one launch (start us, length us, event | category | flops | bytes accessed | tf_op | source)
XLA Modules:
  0.0 18.8 jit_solution(13536846791559631499)
XLA Ops:
  0.0 17.5 %shard_map.73 = f32[32,64]{1,0:T(8,128)} custom-call(s32[1,8]{1,0:T(1,128)} %counts_ref.1, s32[1,64]{1,0:T(1,128)} %bitcast.7, bf16[48,3584]{1,0:T(8,128)(2,1)} %act_hbm.1, bf16[48,2048]{1,0:T(8,128)(2,1)} %grad_hbm.1, bf16[64,3584]{1,0:T(8,128)(2,1)} %bitcast.4, bf16[64,2048]{1,0:T(8,128)(2,1)} %bitcast.5, bf16[8,2,32,256]{3,2,1,0:T(8,128)(2,1)} %bitcast.6), custom_call_target="tpu_custom_call" | custom-call | tf_op jit(solution)/shard_map/pallas_call | solution.py:221
  17.5 1.3 %copy.9 = f32[32,64]{1,0:T(8,128)} copy(f32[32,64]{1,0:T(8,128)} %shard_map.73) | data formatting | bytes 16384

commit v3 on v2

--- a/solution.py
+++ b/solution.py
@@ -64,9 +64,9 @@
 
 def kernel(
     n, chunks,
-    counts_ref, slots_ref, act_hbm, grad_hbm, pin_hbm, pout_hbm, q_hbm, o_ref,
-    act, grad, pin, pout, q, mine, other, g_send, g_recv, s_send, s_recv,
-    in_sems, q_sems, pair_sems, g_send_sems, g_recv_sems, s_send_sems, s_recv_sems,
+    counts_hbm, slots_hbm, act_hbm, grad_hbm, pin_hbm, pout_hbm, q_hbm, o_ref,
+    counts_ref, slots_ref, act, grad, pin, pout, q, mine, other, g_send, g_recv, s_send, s_recv,
+    small_sems, in_sems, q_sems, pair_sems, g_send_sems, g_recv_sems, s_send_sems, s_recv_sems,
 ):
     me = lax.axis_index("dp")
     core = lax.axis_index("cuts")
@@ -75,6 +75,11 @@
     docs = counts_ref.shape[1]
     groups = g_recv.shape[1] // docs
     all_docs = n * docs
+
+    barrier = pltpu.get_barrier_semaphore()
+    pl.semaphore_signal(barrier, inc=1, device_id={"cuts": 1 - core}, device_id_type=MESH)
+    for step in range(1, n):
+        pl.semaphore_signal(barrier, inc=1, device_id={"dp": lax.rem(me + step, n)}, device_id_type=MESH)
 
     loads = []
     for a_hbm, a, p_hbm, p, count in ((act_hbm, act, pin_hbm, pin, chunks[0]), (grad_hbm, grad, pout_hbm, pout, chunks[1])):
@@ -89,14 +94,40 @@
             for copy in pair:
                 copy.start()
             loads.append((pair, a, p, at))
+    small = (
+        pltpu.make_async_copy(counts_hbm, counts_ref, small_sems.at[0]),
+        pltpu.make_async_copy(slots_hbm, slots_ref, small_sems.at[1]),
+    )
+    for copy in small:
+        copy.start()
     q_own = pltpu.make_async_copy(q_hbm.at[:, core], q.at[core], q_sems.at[0])
     q_own.start()
 
-    barrier = pltpu.get_barrier_semaphore()
-    pl.semaphore_signal(barrier, inc=1, device_id={"cuts": 1 - core}, device_id_type=MESH)
-    for step in range(1, n):
-        pl.semaphore_signal(barrier, inc=1, device_id={"dp": lax.rem(me + step, n)}, device_id_type=MESH)
-
+    inward = jnp.zeros((rows, rank), jnp.float32)
+    outward = jnp.zeros((rows, rank), jnp.float32)
+    for number, (pair, a, p, at) in enumerate(loads):
+        for copy in pair:
+            copy.wait()
+        product = dot_nt(a[:, at], p[:, at])
+        if number < chunks[0]:
+            inward = inward + product
+        else:
+            outward = outward + product
+    mine[...] = jnp.concatenate([inward, outward], axis=1)
+
+    pl.semaphore_wait(barrier, n)
+    pair_copy = pltpu.make_async_remote_copy(
+        src_ref=mine, dst_ref=other, send_sem=pair_sems.at[0], recv_sem=pair_sems.at[1],
+        device_id={"cuts": 1 - core}, device_id_type=MESH,
+    )
+    pair_copy.start()
+    q_pair = pltpu.make_async_remote_copy(
+        src_ref=q_hbm.at[:, 1 - core], dst_ref=q.at[core], send_sem=q_sems.at[1], recv_sem=q_sems.at[2],
+        device_id={"cuts": 1 - core}, device_id_type=MESH,
+    )
+    q_pair.start()
+    for copy in small:
+        copy.wait()
     doc_of = lax.broadcasted_iota(jnp.int32, (docs, rows), 0)
     position = lax.broadcasted_iota(jnp.int32, (docs, rows), 1)
     first = jnp.zeros((docs, rows), jnp.int32)
@@ -113,29 +144,6 @@
     column = jnp.where(column >= all_docs, column - all_docs, column)
     place = jnp.where(column == slots_ref[...], 1.0, 0.0).astype(jnp.bfloat16)
 
-    inward = jnp.zeros((rows, rank), jnp.float32)
-    outward = jnp.zeros((rows, rank), jnp.float32)
-    for number, (pair, a, p, at) in enumerate(loads):
-        for copy in pair:
-            copy.wait()
-        product = dot_nt(a[:, at], p[:, at])
-        if number < chunks[0]:
-            inward = inward + product
-        else:
-            outward = outward + product
-    mine[...] = jnp.concatenate([inward, outward], axis=1)
-
-    pl.semaphore_wait(barrier, n)
-    pair_copy = pltpu.make_async_remote_copy(
-        src_ref=mine, dst_ref=other, send_sem=pair_sems.at[0], recv_sem=pair_sems.at[1],
-        device_id={"cuts": 1 - core}, device_id_type=MESH,
-    )
-    pair_copy.start()
-    q_pair = pltpu.make_async_remote_copy(
-        src_ref=q_hbm.at[:, 1 - core], dst_ref=q.at[core], send_sem=q_sems.at[1], recv_sem=q_sems.at[2],
-        device_id={"cuts": 1 - core}, device_id_type=MESH,
-    )
-    q_pair.start()
     pair_copy.wait_recv()
     both = mine[...] + other[...]
 
@@ -220,14 +228,14 @@
     bf16, f32 = jnp.bfloat16, jnp.float32
     return pl.pallas_call(
         functools.partial(kernel, n, chunks),
-        out_shape=jax.ShapeDtypeStruct((out_rows, all_docs), f32),
+        out_shape=pltpu.VMEM((out_rows, all_docs), f32),
         in_specs=[
-            pl.BlockSpec(memory_space=pltpu.SMEM),
-            pl.BlockSpec(memory_space=pltpu.VMEM),
-            anywhere, anywhere, anywhere, anywhere, anywhere,
+            anywhere, anywhere, anywhere, anywhere, anywhere, anywhere, anywhere,
         ],
         out_specs=pl.BlockSpec(memory_space=pltpu.VMEM),
         scratch_shapes=[
+            pltpu.SMEM((1, docs), jnp.int32),
+            pltpu.VMEM((1, all_docs), jnp.int32),
             pltpu.VMEM(activations.shape, bf16),
             pltpu.VMEM(out_grads.shape, bf16),
             pltpu.VMEM(proj_in.shape[::-1], bf16),
@@ -239,6 +247,7 @@
             pltpu.VMEM((n, block, LANES), bf16),
             pltpu.VMEM((n, out_rows // 2, 2 * all_docs), f32),
             pltpu.VMEM((n, out_rows // 2, 2 * all_docs), f32),
+            pltpu.SemaphoreType.DMA((2,)),
             pltpu.SemaphoreType.DMA((2 * sum(chunks),)),
             pltpu.SemaphoreType.DMA((3,)),
             pltpu.SemaphoreType.DMA((2,)),

time: 19.1 us -> 17 us (0.89)
  Pallas kernels: 17.5 us -> 16.2 us
  local copies, waits for them, and re-layouts: 1.32 us -> 0.61 us
    pallas_call x1, Pallas kernels: 17.5 us -> 16.2 us  [fused(): pl.pallas_call(functools.partial(kernel, n, chunks), out_shape=pltpu.VMEM...]
    unnamed x1, local copies, waits for them, and re-layouts: 1.32 us -> 0.61 us
where the time goes in v3:
time: 17 us; the launch traced here: 16.8 us
  Pallas kernels  16.2 us (95%)
  local copies, waits for them, and re-layouts  0.61 us (4%)
    pallas_call x1, Pallas kernels, fused(): pl.pallas_call(functools.partial(kernel, n, chunks), out_shape=pltpu.VMEM...  16.2 us
    unnamed x1, local copies, waits for them, and re-layouts  0.61 us

profile of v3, /device:TPU:0, one launch (start us, length us, event | category | flops | bytes accessed | tf_op | source)
XLA Modules:
  0.0 16.8 jit_solution(14350144977088677045)
XLA Ops:
  0.0 16.2 %shard_map.73 = f32[32,64]{1,0:T(8,128)S(1)} custom-call(s32[1,8]{1,0:T(1,128)} %counts_hbm.1, s32[1,64]{1,0:T(1,128)} %bitcast.7, bf16[48,3584]{1,0:T(8,128)(2,1)} %act_hbm.1, bf16[48,2048]{1,0:T(8,128)(2,1)} %grad_hbm.1, bf16[64,3584]{1,0:T(8,128)(2,1)} %bitcast.4, bf16[64,2048]{1,0:T(8,128)(2,1)} %bitcast.5, bf16[8,2,32,256]{3,2,1,0:T(8,128)(2,1)} %bitcast.6), custom_call_target="tpu_custom_call" | custom-call | tf_op jit(solution)/shard_map/pallas_call | solution.py:229
  16.2 0.6 %copy.9 = f32[32,64]{1,0:T(8,128)} copy(f32[32,64]{1,0:T(8,128)S(1)} %shard_map.73) | data formatting | bytes 16384

commit v4 on v3

--- a/solution.py
+++ b/solution.py
@@ -162,7 +162,7 @@
     g_send[...] = gradients.astype(jnp.bfloat16).reshape(g_send.shape)
 
     g_copies = []
-    for step in range(1, n):
+    for step in sorted(range(1, n), key=lambda s: -abs(2 * s - n)):
         peer = lax.rem(me + step, n)
         copy = pltpu.make_async_remote_copy(
             src_ref=g_send.at[peer], dst_ref=g_recv.at[me],
@@ -191,7 +191,7 @@
     s_send[...] = jnp.where(first_half, scores[:, 0], scores[:, 1])
 
     s_copies = []
-    for step in range(1, n):
+    for step in sorted(range(1, n), key=lambda s: -abs(2 * s - n)):
         peer = lax.rem(me + step, n)
         copy = pltpu.make_async_remote_copy(
             src_ref=s_send.at[peer], dst_ref=s_recv.at[me],
@@ -223,7 +223,7 @@
     query_count, width = queries.shape
     out_rows = query_count // (n * cuts)
     block = cuts * width // LANES * docs
-    chunks = (2, 1)
+    chunks = (1, 1)
     anywhere = pl.BlockSpec(memory_space=pltpu.HBM)
     bf16, f32 = jnp.bfloat16, jnp.float32
     return pl.pallas_call(

time: 17 us -> 16.3 us (0.959)
  Pallas kernels: 16.2 us -> 15.5 us
    pallas_call x1, Pallas kernels: 16.2 us -> 15.5 us  [fused(): pl.pallas_call(functools.partial(kernel, n, chunks), out_shape=pltpu.VMEM...]
where the time goes in v4:
time: 16.3 us; the launch traced here: 16.1 us
  Pallas kernels  15.5 us (95%)
  local copies, waits for them, and re-layouts  0.61 us (4%)
    pallas_call x1, Pallas kernels, fused(): pl.pallas_call(functools.partial(kernel, n, chunks), out_shape=pltpu.VMEM...  15.5 us
    unnamed x1, local copies, waits for them, and re-layouts  0.61 us

profile of v4, /device:TPU:0, one launch (start us, length us, event | category | flops | bytes accessed | tf_op | source)
XLA Modules:
  0.0 16.1 jit_solution(17332254035670052838)
XLA Ops:
  0.0 15.5 %shard_map.73 = f32[32,64]{1,0:T(8,128)S(1)} custom-call(s32[1,8]{1,0:T(1,128)} %counts_hbm.1, s32[1,64]{1,0:T(1,128)} %bitcast.7, bf16[48,3584]{1,0:T(8,128)(2,1)} %act_hbm.1, bf16[48,2048]{1,0:T(8,128)(2,1)} %grad_hbm.1, bf16[64,3584]{1,0:T(8,128)(2,1)} %bitcast.4, bf16[64,2048]{1,0:T(8,128)(2,1)} %bitcast.5, bf16[8,2,32,256]{3,2,1,0:T(8,128)(2,1)} %bitcast.6), custom_call_target="tpu_custom_call" | custom-call | tf_op jit(solution)/shard_map/pallas_call | solution.py:229
  15.5 0.6 %copy.9 = f32[32,64]{1,0:T(8,128)} copy(f32[32,64]{1,0:T(8,128)S(1)} %shard_map.73) | data formatting | bytes 16384
